TPU v7x, 512 devices: a whole 4x4x16 slice. The times are simulated.
512 devices in a mesh: term: 32 (over y, x, core), sector: 16 (over z).
Axes of the slice: x: 4, y: 4, z: 16, core: 2. Of those that a mesh axis runs over, the one named last changes fastest.
Arguments:
- wavefunction: bfloat16 [96, 256, 256], P('sector')
- left_operator_blocks: bfloat16 [384, 256, 256], P('term'), may hold values from -0.01953125 to 0.01953125
- right_operator_blocks: bfloat16 [384, 256, 256], P('term'), may hold values from -0.375 to 0.375
- fetch_index: int32 [32, 16, 16], P('term', 'sector'), may hold values from 0 to 5, as said below
- owner_link: int32 [384, 96], P('term', 'sector'), may hold values from 0 to 15, as said below
- lower_roots: bfloat16 [4, 96, 256, 256], P(None, 'sector', 'term')
- level_shift: float32 [4], replicated, may hold values from 0.5 to 2
Outputs:
- sigma: float32 [96, 256, 256], P('sector', 'term')
- correlations: float32 [4], replicated
Inputs may be any that keep to these rules, and one draw needn't show every extreme that they name: `fetch_index`: entry p of every list is a position within the 6 sectors of sector index p. `owner_link`: within the 12 x 6 entries that one device holds, every sector index occurs at least once.
All inputs are finite; a program needn't handle non-finite values.
Results may differ from a plain program's by a relative error of at most 0.0059.
Values may be sent and summed in bfloat16 or wider, within the bound.
A program may use at most 64 MiB of HBM per device.

v0:
```python
import jax
import jax.numpy as jnp
from jax import lax
from jax.sharding import PartitionSpec as P


def per_device(
    wavefunction,
    left_operator_blocks,
    right_operator_blocks,
    fetch_index,
    owner_link,
    lower_roots,
    level_shift,
):
    sec_dev = wavefunction.shape[0]
    block_width = wavefunction.shape[1]
    group_count = fetch_index.shape[2]
    own_requests = fetch_index.reshape(group_count, 1)
    store = lax.all_gather(wavefunction, "sector", axis=0, tiled=True)
    lookup = owner_link * sec_dev + own_requests[:, 0][owner_link]

    def one_sector(column):
        input_sectors = store[column]
        partial_contraction = jnp.einsum(
            "lhm,lmp->lhp", left_operator_blocks, input_sectors, preferred_element_type=jnp.float32
        ).astype(jnp.bfloat16)
        return jnp.einsum(
            "yxz,ysz->xs",
            partial_contraction,
            right_operator_blocks,
            preferred_element_type=jnp.float32,
        )

    partial_value = lax.map(one_sector, jnp.transpose(lookup))
    reduced = lax.psum_scatter(partial_value, "term", scatter_dimension=1, tiled=True)
    row_count = reduced.shape[1]
    row_start = lax.axis_index("term") * row_count
    psi_rows = lax.dynamic_slice_in_dim(wavefunction, row_start, row_count, 1)
    local_correlation = jnp.einsum(
        "ksab,sab->k", lower_roots, psi_rows, preferred_element_type=jnp.float32
    )
    total_cells = lax.axis_size("sector") * sec_dev * block_width * block_width
    correlations = lax.psum(local_correlation, ("term", "sector")) / total_cells
    sigma = reduced + jnp.einsum(
        "k,ksab->sab", level_shift * correlations, lower_roots.astype(jnp.float32)
    )
    return (sigma, correlations)


def solution(mesh):
    return jax.shard_map(
        per_device,
        mesh=mesh,
        in_specs=(
            P("sector", None, None),
            P("term", None, None),
            P("term", None, None),
            P("term", "sector", None),
            P("term", "sector"),
            P(None, "sector", "term", None),
            P(),
        ),
        out_specs=(P("sector", "term", None), P()),
        check_vma=False,
    )
```

profile of v0, /device:TPU:1, one launch (start us, length us, event | category | flops | bytes accessed | tf_op | source)
XLA Modules:
  0.0 328.3 jit_solution(2077307641894323809)
XLA Ops:
  7.2 0.7 all-gather.2.cloned.1.call-update
  8.0 0.8 copy.17
  8.8 0.7 compare_select_fusion.1
  9.4 0.1 copy.18
  9.7 1.2 gather_fusion.1
  11.1 152.4 %all-gather.2.cloned.1.call-done = bf16[96,256,256]{2,1,0:T(8,128)(2,1)} async-done(((bf16[6,256,256]{2,1,0:T(8,128)(2,1)}), bf16[96,256,256]{2,1,0:T(8,128)(2,1)}) %all-gather.2.cloned.1.call-update) | async-done | bytes 12582928 | tf_op jit(solution)/shard_map/all_gather | solution.py:20
  163.5 52.1 %while.10 = (s32[]{:T(128)}, f32[6,256,256]{2,1,0:T(8,128)}, s32[6,12]{1,0:T(8,128)S(1)}, bf16[96,256,256]{2,1,0:T(8,128)(2,1)}, bf16[12,256,256]{2,1,0:T(8,128)...) while((s32[]{:T(128)}, f32[6,256,256]{2,1,0:T(8,128)}, s32[6,12]{1,0:T(8,128)S(1)}, ...), condition=%wide.region_1.2_spmd, body=%wide.region_0.1_spmd.sunk | while | flops 806093888 | bytes 8130845 | solution.py:35
  163.5 5.2 %gather_fusion = bf16[12,256,256]{2,1,0:T(8,128)(2,1)S(1)} fusion(bf16[96,256,256]{2,1,0:T(8,128)(2,1)} %get-tuple-element.119, s32[1024]{0:T(1024)S(1)} %pad_clamp_fusion.3), kind=kCustom, calls=%fused_computation.clone.1 | custom fusion | bytes 3145776 | tf_op jit(solution)/shard_map/while/body/eval_jaxpr/gather | solution.py:24
  168.8 3.4 %fusion.27 = f32[6,256,256]{2,1,0:T(8,128)} fusion(f32[6,256,256]{2,1,0:T(8,128)} %get-tuple-element.110, s32[]{:T(128)S(6)} %copy.38, bf16[12,256,256]{2,1,0:T(8,128)(2,1)} %get-tuple-element.121, bf16[12,256,256]{2,1,0:T(8,128)(2,1)S(1)} %gather_fusion, bf16[12,256,256]{2,1,0:T(8,128)(2,1)S(1)} %get-tuple-element.120), kind=kOutput, calls=%fused_computation.6.clone.1 | convolution fusion | flops 806092800 | bytes 4980740 | tf_op jit(solution)/shard_map/while/body/eval_jaxpr/yxz,ysz->xs/dot_general | solution.py:28
  172.2 5.2 %gather_fusion = bf16[12,256,256]{2,1,0:T(8,128)(2,1)S(1)} fusion(bf16[96,256,256]{2,1,0:T(8,128)(2,1)} %get-tuple-element.119, s32[1024]{0:T(1024)S(1)} %pad_clamp_fusion.3), kind=kCustom, calls=%fused_computation.clone.1 | custom fusion | bytes 3145776 | tf_op jit(solution)/shard_map/while/body/eval_jaxpr/gather | solution.py:24
  177.4 3.5 %fusion.27 = f32[6,256,256]{2,1,0:T(8,128)} fusion(f32[6,256,256]{2,1,0:T(8,128)} %get-tuple-element.110, s32[]{:T(128)S(6)} %copy.38, bf16[12,256,256]{2,1,0:T(8,128)(2,1)} %get-tuple-element.121, bf16[12,256,256]{2,1,0:T(8,128)(2,1)S(1)} %gather_fusion, bf16[12,256,256]{2,1,0:T(8,128)(2,1)S(1)} %get-tuple-element.120), kind=kOutput, calls=%fused_computation.6.clone.1 | convolution fusion | flops 806092800 | bytes 4980740 | tf_op jit(solution)/shard_map/while/body/eval_jaxpr/yxz,ysz->xs/dot_general | solution.py:28
  180.9 5.2 %gather_fusion = bf16[12,256,256]{2,1,0:T(8,128)(2,1)S(1)} fusion(bf16[96,256,256]{2,1,0:T(8,128)(2,1)} %get-tuple-element.119, s32[1024]{0:T(1024)S(1)} %pad_clamp_fusion.3), kind=kCustom, calls=%fused_computation.clone.1 | custom fusion | bytes 3145776 | tf_op jit(solution)/shard_map/while/body/eval_jaxpr/gather | solution.py:24
  186.1 3.4 %fusion.27 = f32[6,256,256]{2,1,0:T(8,128)} fusion(f32[6,256,256]{2,1,0:T(8,128)} %get-tuple-element.110, s32[]{:T(128)S(6)} %copy.38, bf16[12,256,256]{2,1,0:T(8,128)(2,1)} %get-tuple-element.121, bf16[12,256,256]{2,1,0:T(8,128)(2,1)S(1)} %gather_fusion, bf16[12,256,256]{2,1,0:T(8,128)(2,1)S(1)} %get-tuple-element.120), kind=kOutput, calls=%fused_computation.6.clone.1 | convolution fusion | flops 806092800 | bytes 4980740 | tf_op jit(solution)/shard_map/while/body/eval_jaxpr/yxz,ysz->xs/dot_general | solution.py:28
  189.6 5.2 %gather_fusion = bf16[12,256,256]{2,1,0:T(8,128)(2,1)S(1)} fusion(bf16[96,256,256]{2,1,0:T(8,128)(2,1)} %get-tuple-element.119, s32[1024]{0:T(1024)S(1)} %pad_clamp_fusion.3), kind=kCustom, calls=%fused_computation.clone.1 | custom fusion | bytes 3145776 | tf_op jit(solution)/shard_map/while/body/eval_jaxpr/gather | solution.py:24
  194.8 3.4 %fusion.27 = f32[6,256,256]{2,1,0:T(8,128)} fusion(f32[6,256,256]{2,1,0:T(8,128)} %get-tuple-element.110, s32[]{:T(128)S(6)} %copy.38, bf16[12,256,256]{2,1,0:T(8,128)(2,1)} %get-tuple-element.121, bf16[12,256,256]{2,1,0:T(8,128)(2,1)S(1)} %gather_fusion, bf16[12,256,256]{2,1,0:T(8,128)(2,1)S(1)} %get-tuple-element.120), kind=kOutput, calls=%fused_computation.6.clone.1 | convolution fusion | flops 806092800 | bytes 4980740 | tf_op jit(solution)/shard_map/while/body/eval_jaxpr/yxz,ysz->xs/dot_general | solution.py:28
  198.3 5.2 %gather_fusion = bf16[12,256,256]{2,1,0:T(8,128)(2,1)S(1)} fusion(bf16[96,256,256]{2,1,0:T(8,128)(2,1)} %get-tuple-element.119, s32[1024]{0:T(1024)S(1)} %pad_clamp_fusion.3), kind=kCustom, calls=%fused_computation.clone.1 | custom fusion | bytes 3145776 | tf_op jit(solution)/shard_map/while/body/eval_jaxpr/gather | solution.py:24
  203.5 3.4 %fusion.27 = f32[6,256,256]{2,1,0:T(8,128)} fusion(f32[6,256,256]{2,1,0:T(8,128)} %get-tuple-element.110, s32[]{:T(128)S(6)} %copy.38, bf16[12,256,256]{2,1,0:T(8,128)(2,1)} %get-tuple-element.121, bf16[12,256,256]{2,1,0:T(8,128)(2,1)S(1)} %gather_fusion, bf16[12,256,256]{2,1,0:T(8,128)(2,1)S(1)} %get-tuple-element.120), kind=kOutput, calls=%fused_computation.6.clone.1 | convolution fusion | flops 806092800 | bytes 4980740 | tf_op jit(solution)/shard_map/while/body/eval_jaxpr/yxz,ysz->xs/dot_general | solution.py:28
  206.9 5.2 %gather_fusion = bf16[12,256,256]{2,1,0:T(8,128)(2,1)S(1)} fusion(bf16[96,256,256]{2,1,0:T(8,128)(2,1)} %get-tuple-element.119, s32[1024]{0:T(1024)S(1)} %pad_clamp_fusion.3), kind=kCustom, calls=%fused_computation.clone.1 | custom fusion | bytes 3145776 | tf_op jit(solution)/shard_map/while/body/eval_jaxpr/gather | solution.py:24
  212.2 3.4 %fusion.27 = f32[6,256,256]{2,1,0:T(8,128)} fusion(f32[6,256,256]{2,1,0:T(8,128)} %get-tuple-element.110, s32[]{:T(128)S(6)} %copy.38, bf16[12,256,256]{2,1,0:T(8,128)(2,1)} %get-tuple-element.121, bf16[12,256,256]{2,1,0:T(8,128)(2,1)S(1)} %gather_fusion, bf16[12,256,256]{2,1,0:T(8,128)(2,1)S(1)} %get-tuple-element.120), kind=kOutput, calls=%fused_computation.6.clone.1 | convolution fusion | flops 806092800 | bytes 4980740 | tf_op jit(solution)/shard_map/while/body/eval_jaxpr/yxz,ysz->xs/dot_general | solution.py:28
  215.6 0.7 dynamic-slice_bitcast_fusion
  216.4 0.3 convolution_bitcast_fusion
  216.6 103.1 %psum.7 = f32[4]{0:T(128)S(1)} all-reduce(f32[4]{0:T(128)S(1)} %convolution_bitcast_fusion), channel_id=1, replica_groups=mesh['term'=32,'sector'=16] {'term','sector'}, use_global_device_ids=true, to_apply=%region_3.4 | all-reduce | flops 4 | bytes 32 | tf_op jit(solution)/shard_map/psum | solution.py:44
  319.8 0.2 fusion.9
  320.0 1.4 bitcast_add_fusion
  (33 shorter events, 0.5 us)
Async XLA Ops:
  7.2 209.2 %copy-start = (bf16[4,6,8,256]{3,2,1,0:T(8,128)(2,1)S(1)}, bf16[4,6,8,256]{3,2,1,0:T(8,128)(2,1)}, u32[]{:S(2)}) copy-start(bf16[4,6,8,256]{3,2,1,0:T(8,128)(2,1)} %param.14) | copy-start | bytes 294916
  7.2 2.5 copy-start.1
  7.2 156.3 %all-gather.2.cloned.1.call-start = ((), (), s32[]{:S(2)}) async-start(), calls=%async_computation.1 | async-start | bytes 13369344 | tf_op jit(solution)/shard_map/all_gather | solution.py:20
  7.9 312.1 %reduce-scatter.2.cloned.1.call-start = ((), (), s32[]{:S(2)}) async-start(), calls=%async_computation.2 | async-start | bytes 1622016 | tf_op jit(solution)/shard_map/reduce_scatter | solution.py:36
  9.7 153.9 %copy-start.2 = (bf16[12,256,256]{2,1,0:T(8,128)(2,1)S(1)}, bf16[12,256,256]{2,1,0:T(8,128)(2,1)}, u32[]{:S(2)}) copy-start(bf16[12,256,256]{2,1,0:T(8,128)(2,1)} %param.10) | copy-start | bytes 4718596
  215.6 104.2 %copy-start.3 = (f32[4]{0:T(128)S(1)}, f32[4]{0:T(128)}, u32[]{:S(2)}) copy-start(f32[4]{0:T(128)} %param.15) | copy-start | bytes 52
  319.8 1.6 copy-start.4
Sparse Core Ops, SparseCore 0:
  10.1 153.3 all-gather.1
  215.8 97.6 reduce-scatter.1
where the time goes:
time: 329 us; the launch traced here: 328 us
  waiting for transfers between devices  153 us (47%)
  blocking collectives  103 us (31%)
  local copies, waits for them, and re-layouts  34.5 us (10%)
  matrix products  21 us (6%)
  between operations  14.1 us (4%)
    all_gather x1, waiting for transfers between devices, per_device(): store = lax.all_gather(wavefunction, 'sector', axis=0, tiled=True)  152 us
    psum x1, blocking collectives, per_device(): correlations = lax.psum(local_correlation, ('term', 'sector')) / total_cells  103 us
    gather x6, local copies, waits for them, and re-layouts, one_sector(): input_sectors = store[column]  31.3 us
    dot_general x6, matrix products, one_sector(): jnp.einsum('yxz,ysz->xs', partial_contraction, right_operator_blocks, pre...  20.6 us
  transfers between devices with their start and end apart: 2, of which 1 were waited for; matrix products, arithmetic and copies ran while one was open for 1% of the time, Pallas kernels for 0%

commit v1 on v0

--- a/solution.py
+++ b/solution.py
@@ -1,7 +1,18 @@
+import functools
 import jax
 import jax.numpy as jnp
 from jax import lax
 from jax.sharding import PartitionSpec as P
+
+
+def settle_results(tile_in, row_axis):
+    d_next = jnp.concatenate(
+        jax.lax.all_to_all(jnp.stack(jax.lax.psum(1, row_axis) * [tile_in]), row_axis, 0, 0), 0
+    )
+    return d_next
+
+
+step_on_terms = functools.partial(settle_results, row_axis="sector")
 
 
 def per_device(
@@ -17,7 +28,7 @@
     block_width = wavefunction.shape[1]
     group_count = fetch_index.shape[2]
     own_requests = fetch_index.reshape(group_count, 1)
-    store = lax.all_gather(wavefunction, "sector", axis=0, tiled=True)
+    store = step_on_terms(wavefunction)
     lookup = owner_link * sec_dev + own_requests[:, 0][owner_link]
 
     def one_sector(column):

time: 329 us -> 739 us (2.25)
  waiting for transfers between devices: 153 us -> 539 us
  starting transfers between devices: 0.08 us -> 16 us
    all_to_all x0 -> x1, waiting for transfers between devices: none -> 539 us  [settle_results(): jax.lax.all_to_all(jnp.stack(jax.lax.psum(1, row_axis) * [tile_in]), row_...]
    all_gather x1 -> x0, waiting for transfers between devices: 152 us -> none  [per_device(): store = lax.all_gather(wavefunction, 'sector', axis=0, tiled=True)]
    all_to_all x0 -> x1, starting transfers between devices: none -> 15.9 us  [settle_results(): jax.lax.all_to_all(jnp.stack(jax.lax.psum(1, row_axis) * [tile_in]), row_...]
  transfers between devices with their start and end apart: 2 -> 2, of which waited for: 1 -> 1; matrix products, arithmetic and copies ran while one was open for 1% -> 0% of each run, Pallas kernels for 0% -> 0%
where the time goes in v1:
time: 739 us; the launch traced here: 738 us
  waiting for transfers between devices  539 us (73%)
  blocking collectives  106 us (14%)
  local copies, waits for them, and re-layouts  41.3 us (6%)
  matrix products  19.8 us (3%)
  starting transfers between devices  16 us (2%)
  between operations  14.1 us (2%)
    all_to_all x1, waiting for transfers between devices, settle_results(): jax.lax.all_to_all(jnp.stack(jax.lax.psum(1, row_axis) * [tile_in]), row_...  539 us
    psum x1, blocking collectives, per_device(): correlations = lax.psum(local_correlation, ('term', 'sector')) / total_cells  106 us
    gather x6, local copies, waits for them, and re-layouts, one_sector(): input_sectors = store[column]  31.3 us
    dot_general x6, matrix products, one_sector(): jnp.einsum('yxz,ysz->xs', partial_contraction, right_operator_blocks, pre...  19.4 us
    all_to_all x1, starting transfers between devices, settle_results(): jax.lax.all_to_all(jnp.stack(jax.lax.psum(1, row_axis) * [tile_in]), row_...  15.9 us
  transfers between devices with their start and end apart: 2, of which 1 were waited for; matrix products, arithmetic and copies ran while one was open for 0% of the time, Pallas kernels for 0%

profile of v1, /device:TPU:1, one launch (start us, length us, event | category | flops | bytes accessed | tf_op | source)
XLA Modules:
  0.0 738.0 jit_solution(8726470107922474157)
XLA Ops:
  7.2 7.2 stack.2
  14.4 15.9 %all-to-all-start = ((bf16[16,6,256,256]{3,2,1,0:T(8,128)(2,1)}), bf16[16,6,256,256]{3,2,1,0:T(8,128)(2,1)}, u32[]{:S(2)}, u32[]{:S(2)}) async-start(bf16[16,6,256,256]{3,2,1,0:T(8,128)(2,1)} %stack.2), calls=%async_computation | async-start | bytes 25165824 | tf_op jit(solution)/shard_map/all_to_all | solution.py:10
  30.5 0.1 copy.13
  30.7 0.3 copy-done.1
  31.0 1.2 gather_fusion.1
  32.4 539.3 %all-to-all-done = bf16[16,6,256,256]{3,2,1,0:T(8,128)(2,1)} async-done(((bf16[16,6,256,256]{3,2,1,0:T(8,128)(2,1)}), bf16[16,6,256,256]{3,2,1,0:T(8,128)(2,1)}, u32[]{:S(2)}, u32[]{:S(2)}) %all-to-all-start) | async-done | bytes 12582944 | tf_op jit(solution)/shard_map/all_to_all | solution.py:10
  571.6 50.9 %while.10 = (s32[]{:T(128)}, f32[6,256,256]{2,1,0:T(8,128)}, s32[6,12]{1,0:T(8,128)S(1)}, bf16[96,256,256]{2,1,0:T(8,128)(2,1)}, bf16[12,256,256]{2,1,0:T(8,128)...) while((s32[]{:T(128)}, f32[6,256,256]{2,1,0:T(8,128)}, s32[6,12]{1,0:T(8,128)S(1)}, ...), condition=%wide.region_1.2_spmd, body=%wide.region_0.1_spmd.sunk | while | flops 806093888 | bytes 8131345 | solution.py:46
  571.7 5.2 gather_fusion
  576.9 3.2 fusion.27
  580.1 5.2 gather_fusion
  585.4 3.2 fusion.27
  588.6 5.2 gather_fusion
  593.8 3.2 fusion.27
  597.1 5.2 gather_fusion
  602.3 3.2 fusion.27
  605.6 5.2 gather_fusion
  610.8 3.2 fusion.27
  614.0 5.2 gather_fusion
  619.3 3.2 fusion.27
  622.5 0.7 dynamic-slice_bitcast_fusion
  623.3 0.3 convolution_bitcast_fusion
  623.5 106.0 %psum.7 = f32[4]{0:T(128)S(1)} all-reduce(f32[4]{0:T(128)S(1)} %convolution_bitcast_fusion), channel_id=1, replica_groups=mesh['term'=32,'sector'=16] {'term','sector'}, use_global_device_ids=true, to_apply=%region_3.4 | all-reduce | flops 4 | bytes 32 | tf_op jit(solution)/shard_map/psum | solution.py:55
  729.5 0.2 fusion.9
  729.7 1.4 bitcast_add_fusion
  (35 shorter events, 0.6 us)
Async XLA Ops:
  7.2 616.1 %copy-start = (bf16[4,6,8,256]{3,2,1,0:T(8,128)(2,1)S(1)}, bf16[4,6,8,256]{3,2,1,0:T(8,128)(2,1)}, u32[]{:S(2)}) copy-start(bf16[4,6,8,256]{3,2,1,0:T(8,128)(2,1)} %param.14) | copy-start | bytes 294916
  14.4 16.0 %copy-start.2 = (s32[12,6]{0,1:T(8,128)S(1)}, s32[12,6]{0,1:T(8,128)}, u32[]{:S(2)}) copy-start(s32[12,6]{0,1:T(8,128)} %param.13) | copy-start | bytes 868
  14.4 557.3 %all-to-all-start = ((bf16[16,6,256,256]{3,2,1,0:T(8,128)(2,1)}), bf16[16,6,256,256]{3,2,1,0:T(8,128)(2,1)}, u32[]{:S(2)}, u32[]{:S(2)}) async-start(bf16[16,6,256,256]{3,2,1,0:T(8,128)(2,1)} %stack.2), calls=%async_computation | async-start | bytes 25165824 | tf_op jit(solution)/shard_map/all_to_all | solution.py:10
  30.3 0.7 copy-start.1
  30.3 699.4 %reduce-scatter.2.cloned.1.call-start = ((), (), s32[]{:S(2)}) async-start(), calls=%async_computation.2 | async-start | bytes 1622016 | tf_op jit(solution)/shard_map/reduce_scatter | solution.py:47
  31.0 540.7 %copy-start.3 = (bf16[12,256,256]{2,1,0:T(8,128)(2,1)S(1)}, bf16[12,256,256]{2,1,0:T(8,128)(2,1)}, u32[]{:S(2)}) copy-start(bf16[12,256,256]{2,1,0:T(8,128)(2,1)} %param.10) | copy-start | bytes 4718596
  622.5 107.0 %copy-start.4 = (f32[4]{0:T(128)S(1)}, f32[4]{0:T(128)}, u32[]{:S(2)}) copy-start(f32[4]{0:T(128)} %param.15) | copy-start | bytes 52
  729.5 1.6 copy-start.5
Sparse Core Ops, SparseCore 0:
  622.6 100.3 reduce-scatter.1
